TPU v7x, 256 devices: a whole 4x4x8 slice. The times are simulated.
256 devices in a mesh: dp: 4 (over z_hi, core), expert: 64 (over x, y, z_lo).
Axes of the slice: x: 4, y: 4, z: 8 (z_hi: 2, z_lo: 4; z = z_hi * 4 + z_lo), core: 2. Of those that a mesh axis runs over, the one named last changes fastest.
Arguments:
- tokens: bfloat16 [65536, 768], P(('dp', 'expert')), may hold values from -6 to 6
- upstream: bfloat16 [65536, 768], P(('dp', 'expert')), may hold values from -4 to 4
- gate_prob: float32 [65536], P(('dp', 'expert')), may hold values from 0.2 to 1
- expert_id: int32 [65536], P(('dp', 'expert')), may hold values from 0 to 63
- slot_index: int32 [65536], P(('dp', 'expert')), may hold values from -1 to 4, as said below
- segment_id: int32 [256, 256], P(('dp', 'expert')), may hold values from 0 to 3, never falling along the last dimension, each value on 1 to 128 neighbouring positions
- weight_in: bfloat16 [64, 3072, 768], P('expert'), may hold values from -0.21875 to 0.21875
- weight_out: bfloat16 [64, 3072, 768], P('expert'), may hold values from -0.109375 to 0.109375
Outputs:
- d_tokens: bfloat16 [65536, 768], P(('dp', 'expert'))
- d_gate: float32 [65536], P(('dp', 'expert'))
- grad_in: bfloat16 [64, 3072, 768], P('expert', 'dp')
- grad_out: bfloat16 [64, 3072, 768], P('expert', 'dp')
Inputs may be any that keep to these rules, and one draw needn't show every extreme that they name: `slot_index`: -1 marks a dropped token; otherwise the number of earlier tokens of the same row with the same expert_id. A token is dropped exactly when 5 or more earlier tokens of its row chose its expert. `segment_id`: never falling along a row.
All inputs are finite; a program needn't handle non-finite values.
Results may differ from a plain program's by a relative error of at most 0.02.
Values may be sent and summed in bfloat16 or wider, within the bound.
A program may use at most 128 MiB of HBM per device.

v0:
```python
from functools import partial

import jax
import jax.numpy as jnp
from jax import lax
from jax.sharding import PartitionSpec as P

SEGS = 4


def gelu_back(pre_act, grad_rows):
    return jax.vjp(partial(jax.nn.gelu, approximate=True), pre_act)[1](grad_rows)[0]


def pick_rows(values, owners):
    padding = jnp.zeros((1,) + values.shape[1:], values.dtype)
    return jnp.concatenate([values, padding], axis=0)[owners]


def body(tokens, upstream, gate_prob, expert_id, slot_index, segment_id, weight_in, weight_out):
    experts = lax.axis_size("expert")
    tok_rows, model_width = tokens.shape
    hidden_units = weight_in.shape[1]
    capacity = 5 * tok_rows // (4 * experts)
    slots_all = experts * capacity
    first_weight = weight_in[0]
    second_weight = weight_out[0]
    labels = jnp.arange(SEGS, dtype=jnp.int32)
    member = (segment_id[0][:, None] == labels[None, :]).astype(jnp.float32)
    counts = jnp.sum(member, axis=0)
    length = jnp.sum(member * counts[None, :], axis=1)
    doc_weight = tok_rows / (SEGS * length)
    cotangent = (upstream.astype(jnp.float32) * doc_weight[:, None]).astype(jnp.bfloat16)
    position = jnp.where(slot_index >= 0, expert_id * capacity + slot_index, slots_all)
    filled = jnp.full((slots_all + 1,), tok_rows, jnp.int32)
    owners = filled.at[position].set(jnp.arange(tok_rows, dtype=jnp.int32))[:slots_all]
    send_x = pick_rows(tokens, owners).reshape(experts, capacity, model_width)
    send_c = pick_rows(cotangent, owners).reshape(experts, capacity, model_width)
    send_g = pick_rows(gate_prob, owners).reshape(experts, capacity)
    x_part = lax.all_to_all(send_x, "expert", split_axis=0, concat_axis=0, tiled=True)
    c_part = lax.all_to_all(send_c, "expert", split_axis=0, concat_axis=0, tiled=True)
    g_part = lax.all_to_all(
        send_g.astype(jnp.bfloat16), "expert", split_axis=0, concat_axis=0, tiled=True
    ).astype(send_g.dtype)
    pre_act = jnp.einsum("skd,fd->skf", x_part, first_weight, preferred_element_type=jnp.float32)
    hidden = jax.nn.gelu(pre_act, approximate=True).astype(jnp.bfloat16)
    produced = jnp.einsum("skf,fd->skd", hidden, second_weight, preferred_element_type=jnp.float32)
    c_float = c_part.astype(jnp.float32)
    d_gate_rows = jnp.sum(produced * c_float, axis=2)
    d_out = (g_part[:, :, None] * c_float).astype(jnp.bfloat16)
    d_hidden = jnp.einsum("skd,fd->skf", d_out, second_weight, preferred_element_type=jnp.float32)
    d_pre = gelu_back(pre_act, d_hidden).astype(jnp.bfloat16)
    d_in_rows = jnp.einsum(
        "skf,fd->skd", d_pre, first_weight, preferred_element_type=jnp.float32
    ).astype(jnp.bfloat16)
    x_rows, d_in_rows, d_gate_rows, hidden, d_out, d_pre = (
        x_part,
        d_in_rows,
        d_gate_rows,
        hidden,
        d_out,
        d_pre,
    )
    back_rows, back_gate = (
        lax.all_to_all(d_in_rows, "expert", split_axis=0, concat_axis=0, tiled=True),
        lax.all_to_all(
            d_gate_rows.astype(jnp.bfloat16), "expert", split_axis=0, concat_axis=0, tiled=True
        ).astype(d_gate_rows.dtype),
    )
    d_tokens = pick_rows(back_rows.reshape(slots_all, model_width), position)
    d_gate = pick_rows(back_gate.reshape(slots_all), position)
    x_flat = x_rows.reshape(slots_all, model_width)
    d_out_flat = d_out.reshape(slots_all, model_width)
    hidden_flat = hidden.reshape(slots_all, hidden_units)
    d_pre_flat = d_pre.reshape(slots_all, hidden_units)
    columns = d_pre_flat
    grad_first = lax.psum_scatter(
        jnp.einsum("rf,rd->fd", columns, x_flat, preferred_element_type=jnp.float32).astype(
            jnp.bfloat16
        ),
        "dp",
        scatter_dimension=0,
        tiled=True,
    )
    columns = hidden_flat
    grad_second = lax.psum_scatter(
        jnp.einsum("rf,rd->fd", columns, d_out_flat, preferred_element_type=jnp.float32).astype(
            jnp.bfloat16
        ),
        "dp",
        scatter_dimension=0,
        tiled=True,
    )
    return (d_tokens, d_gate, grad_first[None], grad_second[None])


def solution(mesh):
    in_specs = (
        P(("dp", "expert"), None),
        P(("dp", "expert"), None),
        P(("dp", "expert")),
        P(("dp", "expert")),
        P(("dp", "expert")),
        P(("dp", "expert"), None),
        P("expert", None, None),
        P("expert", None, None),
    )
    out_specs = (
        P(("dp", "expert"), None),
        P(("dp", "expert")),
        P("expert", "dp", None),
        P("expert", "dp", None),
    )
    return jax.shard_map(body, mesh=mesh, in_specs=in_specs, out_specs=out_specs, check_vma=False)
```

profile of v0, /device:TPU:1, one launch (start us, length us, event | category | flops | bytes accessed | tf_op | source)
XLA Modules:
  0.0 290.5 jit_solution(15537389992782908054)
XLA Ops:
  7.9 1.4 scatter_custom_fusion
  10.0 2.5 gather_fusion
  13.2 12.6 %all-to-all-start = ((bf16[64,1,5]{2,1,0:T(2,128)(2,1)}), bf16[64,1,5]{2,1,0:T(2,128)(2,1)S(1)}, u32[]{:S(2)}, u32[]{:S(2)}) async-start(bf16[64,1,5]{2,1,0:T(2,128)(2,1)} %convert_element_type.89), calls=%async_computation | async-start | bytes 65536 | tf_op jit(solution)/shard_map/all_to_all | solution.py:42
  26.9 2.1 gather_fusion.2
  30.1 4.3 %all-to-all-done = bf16[64,1,5]{2,1,0:T(2,128)(2,1)S(1)} async-done(((bf16[64,1,5]{2,1,0:T(2,128)(2,1)}), bf16[64,1,5]{2,1,0:T(2,128)(2,1)S(1)}, u32[]{:S(2)}, u32[]{:S(2)}) %all-to-all-start) | async-done | bytes 672 | tf_op jit(solution)/shard_map/all_to_all | solution.py:42
  34.4 5.8 %all-to-all-start.2 = ((bf16[64,5,768]{2,1,0:T(8,128)(2,1)}), bf16[64,5,768]{2,1,0:T(8,128)(2,1)S(1)}, u32[]{:S(2)}, u32[]{:S(2)}) async-start(bf16[64,5,768]{2,1,0:T(8,128)(2,1)} %reshape.63), calls=%async_computation.2 | async-start | bytes 1572864 | tf_op jit(solution)/shard_map/all_to_all | solution.py:40
  40.6 2.1 gather_fusion.1
  43.8 19.2 %all-to-all-done.2 = bf16[64,5,768]{2,1,0:T(8,128)(2,1)S(1)} async-done(((bf16[64,5,768]{2,1,0:T(8,128)(2,1)}), bf16[64,5,768]{2,1,0:T(8,128)(2,1)S(1)}, u32[]{:S(2)}, u32[]{:S(2)}) %all-to-all-start.2) | async-done | bytes 491552 | tf_op jit(solution)/shard_map/all_to_all | solution.py:40
  63.0 4.8 %all-to-all-start.1 = ((bf16[64,5,768]{2,1,0:T(8,128)(2,1)}), bf16[64,5,768]{2,1,0:T(8,128)(2,1)S(1)}, u32[]{:S(2)}, u32[]{:S(2)}) async-start(bf16[64,5,768]{2,1,0:T(8,128)(2,1)} %reshape.62), calls=%async_computation.1 | async-start | bytes 1572864 | tf_op jit(solution)/shard_map/all_to_all | solution.py:41
  68.0 6.0 %fusion.2 = f32[64,5,3072]{2,0,1:T(8,128)} fusion(bf16[1,3072,768]{2,1,0:T(8,128)(2,1)} %param.14, bf16[64,5,768]{2,1,0:T(8,128)(2,1)S(1)} %all-to-all-done.2), kind=kOutput, calls=%fused_computation.12 | convolution fusion | flops 1509949440 | bytes 9142272 | tf_op jit(solution)/shard_map/skd,fd->skf/dot_general | solution.py:45
  74.0 16.5 %all-to-all-done.1 = bf16[64,5,768]{2,1,0:T(8,128)(2,1)S(1)} async-done(((bf16[64,5,768]{2,1,0:T(8,128)(2,1)}), bf16[64,5,768]{2,1,0:T(8,128)(2,1)S(1)}, u32[]{:S(2)}, u32[]{:S(2)}) %all-to-all-start.1) | async-done | bytes 491552 | tf_op jit(solution)/shard_map/all_to_all | solution.py:41
  90.5 7.3 %bitcast_convert_fusion = bf16[3072,768]{1,0:T(8,128)(2,1)} fusion(f32[64,5]{0,1:T(8,128)S(1)} %copy.24, bf16[64,5,768]{2,1,0:T(8,128)(2,1)S(1)} %all-to-all-done.1, f32[64,5,3072]{2,0,1:T(8,128)} %fusion.2), kind=kOutput, calls=%fused_computation.6 | convolution fusion | flops 1521893376 | bytes 9143552 | tf_op jit(solution)/shard_map/rf,rd->fd/dot_general | solution.py:87
  98.1 7.2 %fusion.14 = bf16[64,5,3072]{2,0,1:T(8,128)(2,1)S(1)} fusion(f32[64,5,3072]{2,0,1:T(8,128)} %fusion.2, bf16[1,3072,768]{2,1,0:T(8,128)(2,1)} %param.15, f32[64,5]{0,1:T(8,128)S(1)} %copy.24, bf16[64,5,768]{2,1,0:T(8,128)(2,1)S(1)} %all-to-all-done.1), kind=kOutput, calls=%fused_computation.24 | convolution fusion | flops 1530347520 | bytes 11109632 | tf_op jit(solution)/shard_map/skd,fd->skf/dot_general | solution.py:51
  105.3 4.4 %bitcast_convert_fusion.1 = bf16[3072,768]{1,0:T(8,128)(2,1)} fusion(bf16[64,5,3072]{2,0,1:T(8,128)(2,1)S(1)} %fusion.14, bf16[64,5,768]{2,1,0:T(8,128)(2,1)S(1)} %all-to-all-done.2), kind=kOutput, calls=%fused_computation.7 | convolution fusion | flops 1512308736 | bytes 7176192 | tf_op jit(solution)/shard_map/rf,rd->fd/dot_general | solution.py:78
  109.7 6.9 %fusion.23 = bf16[64,5]{0,1:T(8,128)(2,1)S(1)} fusion(bf16[1,3072,768]{2,1,0:T(8,128)(2,1)} %param.15, bf16[64,5,768]{2,1,0:T(8,128)(2,1)S(1)} %all-to-all-done.1, f32[64,5,3072]{2,0,1:T(8,128)} %fusion.2), kind=kOutput, calls=%fused_computation.28 | convolution fusion | flops 1519533824 | bytes 9142912 | tf_op jit(solution)/shard_map/skf,fd->skd/dot_general | solution.py:47
  117.3 5.0 %all-to-all-start.4 = ((bf16[64,1,5]{2,1,0:T(2,128)(2,1)}), bf16[64,1,5]{2,1,0:T(2,128)(2,1)S(1)}, u32[]{:S(2)}, u32[]{:S(2)}) async-start(bf16[64,1,5]{2,1,0:T(2,128)(2,1)} %copy.28), calls=%async_computation.4 | async-start | bytes 65536 | tf_op jit(solution)/shard_map/all_to_all | solution.py:66
  122.4 4.1 %fusion.20 = bf16[64,5,768]{2,0,1:T(8,128)(2,1)S(1)} fusion(bf16[64,5,3072]{2,0,1:T(8,128)(2,1)S(1)} %fusion.14, bf16[1,3072,768]{2,1,0:T(8,128)(2,1)} %param.14), kind=kOutput, calls=%fused_computation.27 | convolution fusion | flops 1510195200 | bytes 7176192 | tf_op jit(solution)/shard_map/skf,fd->skd/dot_general | solution.py:53
  126.5 1.2 copy.27
  127.6 3.4 %all-to-all-done.4 = bf16[64,1,5]{2,1,0:T(2,128)(2,1)S(1)} async-done(((bf16[64,1,5]{2,1,0:T(2,128)(2,1)}), bf16[64,1,5]{2,1,0:T(2,128)(2,1)S(1)}, u32[]{:S(2)}, u32[]{:S(2)}) %all-to-all-start.4) | async-done | bytes 672 | tf_op jit(solution)/shard_map/all_to_all | solution.py:66
  131.0 6.7 %all-to-all-start.3 = ((bf16[64,5,768]{2,1,0:T(8,128)(2,1)}), bf16[64,5,768]{2,1,0:T(8,128)(2,1)S(1)}, u32[]{:S(2)}, u32[]{:S(2)}) async-start(bf16[64,5,768]{2,1,0:T(8,128)(2,1)} %copy.27), calls=%async_computation.3 | async-start | bytes 1572864 | tf_op jit(solution)/shard_map/all_to_all | solution.py:65
  138.0 2.5 gather_fusion.4
  140.6 59.4 %all-to-all-done.3 = bf16[64,5,768]{2,1,0:T(8,128)(2,1)S(1)} async-done(((bf16[64,5,768]{2,1,0:T(8,128)(2,1)}), bf16[64,5,768]{2,1,0:T(8,128)(2,1)S(1)}, u32[]{:S(2)}, u32[]{:S(2)}) %all-to-all-start.3) | async-done | bytes 491552 | tf_op jit(solution)/shard_map/all_to_all | solution.py:65
  200.3 1.9 gather_fusion.3
  202.2 81.5 %reduce-scatter.3.cloned.1.call-done = bf16[768,768]{1,0:T(8,128)(2,1)} async-done(((bf16[3072,768]{1,0:T(8,128)(2,1)}), bf16[768,768]{1,0:T(8,128)(2,1)}) %reduce-scatter.3.cloned.1.call-update) | async-done | bytes 1179664 | tf_op jit(solution)/shard_map/reduce_scatter | solution.py:77
  (32 shorter events, 7.5 us)
Async XLA Ops:
  13.2 21.1 %all-to-all-start = ((bf16[64,1,5]{2,1,0:T(2,128)(2,1)}), bf16[64,1,5]{2,1,0:T(2,128)(2,1)S(1)}, u32[]{:S(2)}, u32[]{:S(2)}) async-start(bf16[64,1,5]{2,1,0:T(2,128)(2,1)} %convert_element_type.89), calls=%async_computation | async-start | bytes 65536 | tf_op jit(solution)/shard_map/all_to_all | solution.py:42
  25.8 14.4 %copy-start.1 = (s32[1,256]{1,0:T(1,128)S(1)}, s32[1,256]{1,0:T(1,128)}, u32[]{:S(2)}) copy-start(s32[1,256]{1,0:T(1,128)} %param.13) | copy-start | bytes 3076
  25.8 14.6 %copy-start = (bf16[256,768]{1,0:T(8,128)(2,1)S(1)}, bf16[256,768]{1,0:T(8,128)(2,1)}, u32[]{:S(2)}) copy-start(bf16[256,768]{1,0:T(8,128)(2,1)} %param.9) | copy-start | bytes 1179652
  34.4 28.6 %all-to-all-start.2 = ((bf16[64,5,768]{2,1,0:T(8,128)(2,1)}), bf16[64,5,768]{2,1,0:T(8,128)(2,1)S(1)}, u32[]{:S(2)}, u32[]{:S(2)}) async-start(bf16[64,5,768]{2,1,0:T(8,128)(2,1)} %reshape.63), calls=%async_computation.2 | async-start | bytes 1572864 | tf_op jit(solution)/shard_map/all_to_all | solution.py:40
  63.0 27.5 %all-to-all-start.1 = ((bf16[64,5,768]{2,1,0:T(8,128)(2,1)}), bf16[64,5,768]{2,1,0:T(8,128)(2,1)S(1)}, u32[]{:S(2)}, u32[]{:S(2)}) async-start(bf16[64,5,768]{2,1,0:T(8,128)(2,1)} %reshape.62), calls=%async_computation.1 | async-start | bytes 1572864 | tf_op jit(solution)/shard_map/all_to_all | solution.py:41
  67.8 134.4 %reduce-scatter.5.cloned.1.call-start = ((), (), s32[]{:S(2)}) async-start(), calls=%async_computation.8 | async-start | bytes 5898240 | tf_op jit(solution)/shard_map/reduce_scatter | solution.py:86
  97.8 185.8 %reduce-scatter.3.cloned.1.call-start = ((), (), s32[]{:S(2)}) async-start(), calls=%async_computation.7 | async-start | bytes 5898240 | tf_op jit(solution)/shard_map/reduce_scatter | solution.py:77
  117.3 13.6 %all-to-all-start.4 = ((bf16[64,1,5]{2,1,0:T(2,128)(2,1)}), bf16[64,1,5]{2,1,0:T(2,128)(2,1)S(1)}, u32[]{:S(2)}, u32[]{:S(2)}) async-start(bf16[64,1,5]{2,1,0:T(2,128)(2,1)} %copy.28), calls=%async_computation.4 | async-start | bytes 65536 | tf_op jit(solution)/shard_map/all_to_all | solution.py:66
  131.0 69.0 %all-to-all-start.3 = ((bf16[64,5,768]{2,1,0:T(8,128)(2,1)}), bf16[64,5,768]{2,1,0:T(8,128)(2,1)S(1)}, u32[]{:S(2)}, u32[]{:S(2)}) async-start(bf16[64,5,768]{2,1,0:T(8,128)(2,1)} %copy.27), calls=%async_computation.3 | async-start | bytes 1572864 | tf_op jit(solution)/shard_map/all_to_all | solution.py:65
Sparse Core Ops, SparseCore 0:
  98.0 96.3 reduce-scatter.4
  198.0 85.6 reduce-scatter.2
where the time goes:
time: 291 us
  waiting for transfers between devices  184 us (63%)
  matrix products  35.9 us (12%)
  starting transfers between devices  35.2 us (12%)
  local copies, waits for them, and re-layouts  18.9 us (6%)
  between operations  14.2 us (5%)
    reduce_scatter x1, waiting for transfers between devices, body(): lax.psum_scatter(jnp.einsum('rf,rd->fd', columns, x_flat, preferred_eleme...  81.5 us
    all_to_all x1, waiting for transfers between devices, body(): lax.all_to_all(d_in_rows, 'expert', split_axis=0, concat_axis=0, tiled=True)  59.4 us
    all_to_all x1, waiting for transfers between devices, body(): lax.all_to_all(send_x, 'expert', split_axis=0, concat_axis=0, tiled=True)  19.2 us
    all_to_all x1, waiting for transfers between devices, body(): lax.all_to_all(send_c, 'expert', split_axis=0, concat_axis=0, tiled=True)  16.5 us
    all_to_all x1, starting transfers between devices, body(): lax.all_to_all(send_g.astype(jnp.bfloat16), 'expert', split_axis=0, conca...  12.6 us
    gather x5, local copies, waits for them, and re-layouts, pick_rows(): return jnp.concatenate([values, padding], axis=0)[owners]  11.1 us
    dot_general x1, matrix products, body(): jnp.einsum('rf,rd->fd', columns, d_out_flat, preferred_element_type=jnp.f...  7.28 us
    dot_general x1, matrix products, body(): jnp.einsum('skd,fd->skf', d_out, second_weight, preferred_element_type=jn...  7.24 us
  transfers between devices with their start and end apart: 7, of which 6 were waited for; matrix products, arithmetic and copies ran while one was open for 15% of the time, Pallas kernels for 0%

commit v1 on v0

v1 whole, which is shorter than its diff:
```python
from functools import partial

import jax
import jax.numpy as jnp
from jax import lax
from jax.sharding import PartitionSpec as P

SEGS = 4
BF = jnp.bfloat16
F32 = jnp.float32


def gelu_back(pre_act, grad_rows):
    return jax.vjp(partial(jax.nn.gelu, approximate=True), pre_act)[1](grad_rows)[0]


def mm(spec, a, b):
    return jnp.einsum(spec, a, b, preferred_element_type=F32)


def body(tokens, upstream, gate_prob, expert_id, slot_index, segment_id, weight_in, weight_out):
    experts = lax.axis_size("expert")
    groups = lax.axis_size("dp")
    tok_rows, width = tokens.shape
    hidden_units = weight_in.shape[1]
    capacity = 5 * tok_rows // (4 * experts)
    slots_all = experts * capacity
    own_units = hidden_units // groups
    w_in = weight_in[0]
    w_out = weight_out[0]
    labels = jnp.arange(SEGS, dtype=jnp.int32)
    member = (segment_id[0][:, None] == labels[None, :]).astype(F32)
    counts = jnp.sum(member, axis=0)
    length = jnp.sum(member * counts[None, :], axis=1)
    doc_weight = tok_rows / (SEGS * length)
    cotangent = (upstream.astype(F32) * doc_weight[:, None]).astype(BF)
    d_out_tok = (gate_prob[:, None] * cotangent.astype(F32)).astype(BF)
    position = jnp.where(slot_index >= 0, expert_id * capacity + slot_index, slots_all)
    one_hot = (position[None, :] == jnp.arange(slots_all, dtype=jnp.int32)[:, None]).astype(BF)
    both = jnp.concatenate([tokens, d_out_tok], axis=1)
    sent = mm("st,td->sd", one_hot, both).astype(BF)
    sent = sent.reshape(experts, capacity * 2 * width // 256, 256)
    got = lax.all_to_all(sent, "expert", split_axis=0, concat_axis=0, tiled=True)
    rows = got.reshape(slots_all, 2 * width)
    every = lax.all_gather(rows, "dp", axis=0, tiled=True)
    x_own, d_own = rows[:, :width], rows[:, width:]
    pre = mm("rd,fd->rf", x_own, w_in)
    hidden = jax.nn.gelu(pre, approximate=True).astype(BF)
    d_hidden = mm("rd,fd->rf", d_own, w_out)
    gate_sum = jnp.sum(hidden.astype(F32) * d_hidden, axis=1)
    d_pre = gelu_back(pre, d_hidden).astype(BF)
    d_in = mm("rf,fd->rd", d_pre, w_in).astype(BF)
    gate_high = gate_sum.astype(BF)
    gate_low = (gate_sum - gate_high.astype(F32)).astype(BF)
    gates = jnp.concatenate(
        [
            gate_high.reshape(experts, 1, capacity),
            gate_low.reshape(experts, 1, capacity),
            jnp.zeros((experts, 1, 256 - 2 * capacity), BF),
        ],
        axis=2,
    )
    back = jnp.concatenate([d_in.reshape(experts, capacity * width // 256, 256), gates], axis=1)
    returned = lax.all_to_all(back, "expert", split_axis=0, concat_axis=0, tiled=True)
    back_rows = returned[:, :-1].reshape(slots_all, width)
    back_high = returned[:, -1, :capacity].astype(F32).reshape(slots_all)
    back_low = returned[:, -1, capacity : 2 * capacity].astype(F32).reshape(slots_all)
    d_tokens = mm("st,sd->td", one_hot, back_rows).astype(BF)
    hot = one_hot.astype(F32)
    d_gate = jnp.sum(hot * (back_high + back_low)[:, None], axis=0) / gate_prob
    start = lax.axis_index("dp") * own_units
    w_in_q = lax.dynamic_slice_in_dim(w_in, start, own_units, 0)
    w_out_q = lax.dynamic_slice_in_dim(w_out, start, own_units, 0)
    x_all, d_all = every[:, :width], every[:, width:]
    pre_q = mm("rd,fd->rf", x_all, w_in_q)
    hidden_q = jax.nn.gelu(pre_q, approximate=True).astype(BF)
    d_pre_q = gelu_back(pre_q, mm("rd,fd->rf", d_all, w_out_q)).astype(BF)
    grad_in = mm("rf,rd->fd", d_pre_q, x_all).astype(BF)
    grad_out = mm("rf,rd->fd", hidden_q, d_all).astype(BF)
    return (d_tokens, d_gate, grad_in[None], grad_out[None])


def solution(mesh):
    in_specs = (
        P(("dp", "expert"), None),
        P(("dp", "expert"), None),
        P(("dp", "expert")),
        P(("dp", "expert")),
        P(("dp", "expert")),
        P(("dp", "expert"), None),
        P("expert", None, None),
        P("expert", None, None),
    )
    out_specs = (
        P(("dp", "expert"), None),
        P(("dp", "expert")),
        P("expert", "dp", None),
        P("expert", "dp", None),
    )
    return jax.shard_map(body, mesh=mesh, in_specs=in_specs, out_specs=out_specs, check_vma=False)
```

time: 291 us -> 161 us (0.55)
  waiting for transfers between devices: 184 us -> 55.1 us
  blocking collectives: 0 us -> 40.7 us
  starting transfers between devices: 35.2 us -> 5.24 us
  local copies, waits for them, and re-layouts: 18.9 us -> 4.04 us
  other arithmetic: 1.97 us -> 5.41 us
    reduce_scatter x2 -> x0, waiting for transfers between devices: 81.5 us -> none  [the longest x1 81.5 us: body(): lax.psum_scatter(jnp.einsum('rf,rd->fd', columns, x_flat, preferred_eleme...]
    all_to_all x5 -> x1, waiting for transfers between devices: 103 us -> 55.1 us  [body(): lax.all_to_all(back, 'expert', split_axis=0, concat_axis=0, tiled=True)]
    all_to_all x0 -> x1, blocking collectives: none -> 40.7 us  [body(): lax.all_to_all(sent, 'expert', split_axis=0, concat_axis=0, tiled=True)]
    all_to_all x5 -> x1, starting transfers between devices: 34.9 us -> 5.2 us  [body(): lax.all_to_all(back, 'expert', split_axis=0, concat_axis=0, tiled=True)]
    gather x5 -> x0, local copies, waits for them, and re-layouts: 11.1 us -> none  [pick_rows(): return jnp.concatenate([values, padding], axis=0)[owners]]
    dot_general x6 -> x8, matrix products: 35.9 us -> 35.7 us  [mm(): return jnp.einsum(spec, a, b, preferred_element_type=F32)]
  transfers between devices with their start and end apart: 7 -> 2, of which waited for: 6 -> 1; matrix products, arithmetic and copies ran while one was open for 15% -> 9% of each run, Pallas kernels for 0% -> 0%
where the time goes in v1:
time: 161 us; the launch traced here: 160 us
  waiting for transfers between devices  55.1 us (34%)
  blocking collectives  40.7 us (25%)
  matrix products  35.7 us (22%)
  between operations  14.2 us (9%)
  other arithmetic  5.41 us (3%)
  starting transfers between devices  5.24 us (3%)
  local copies, waits for them, and re-layouts  4.04 us (3%)
    all_to_all x1, waiting for transfers between devices, body(): lax.all_to_all(back, 'expert', split_axis=0, concat_axis=0, tiled=True)  55.1 us
    all_to_all x1, blocking collectives, body(): lax.all_to_all(sent, 'expert', split_axis=0, concat_axis=0, tiled=True)  40.7 us
    dot_general x8, matrix products, mm(): return jnp.einsum(spec, a, b, preferred_element_type=F32)  35.7 us
    all_to_all x1, starting transfers between devices, body(): lax.all_to_all(back, 'expert', split_axis=0, concat_axis=0, tiled=True)  5.2 us
  transfers between devices with their start and end apart: 2, of which 1 were waited for; matrix products, arithmetic and copies ran while one was open for 9% of the time, Pallas kernels for 0%

profile of v1, /device:TPU:1, one launch (start us, length us, event | category | flops | bytes accessed | tf_op | source)
XLA Modules:
  0.0 160.4 jit_solution(17310538478647212979)
XLA Ops:
  7.2 0.8 convert_reduce_fusion
  8.0 0.8 select_reduce_fusion
  8.8 0.7 compare_select_fusion
  9.5 1.2 multiply_convert_fusion.7
  10.7 1.4 convolution_convert_fusion
  12.1 0.9 reshape.79
  13.0 40.7 %all_to_all.10 = bf16[64,30,256]{2,1,0:T(8,128)(2,1)S(1)} all-to-all(bf16[64,30,256]{2,1,0:T(8,128)(2,1)S(1)} %reshape.79), channel_id=1, replica_groups=mesh['dp'=4,'expert'=64] {'expert'}, dimensions={0} | all-to-all | bytes 1966080 | tf_op jit(solution)/shard_map/all_to_all | solution.py:43
  53.8 1.9 %reshape.80 = bf16[320,1536]{1,0:T(8,128)(2,1)} reshape(bf16[64,30,256]{2,1,0:T(8,128)(2,1)S(1)} %all_to_all.10) | data formatting | bytes 1966080 | tf_op jit(solution)/shard_map/reshape | solution.py:44
  55.7 4.3 %fusion.2 = f32[320,3072]{1,0:T(8,128)S(1)} fusion(bf16[1,3072,768]{2,1,0:T(8,128)(2,1)} %param.14, bf16[320,1536]{1,0:T(8,128)(2,1)} %reshape.80), kind=kOutput, calls=%fused_computation.6 | convolution fusion | flops 1509949440 | bytes 9142272 | tf_op jit(solution)/shard_map/rd,fd->rf/dot_general | solution.py:18
  60.1 2.1 %multiply_reduce_fusion = (f32[320]{0:T(512)S(1)}, f32[320,3072]{1,0:T(8,128)S(1)}) fusion(f32[320,3072]{1,0:T(8,128)S(1)} %fusion.2, bf16[1,3072,768]{2,1,0:T(8,128)(2,1)S(1)} %copy-done.2, bf16[320,1536]{1,0:T(8,128)(2,1)S(1)} %copy-done), kind=kOutput, calls=%fused_computation.25 | convolution fusion | flops 1521745664 | bytes 13075712 | tf_op jit(solution)/shard_map/rd,fd->rf/dot_general | solution.py:18
  62.3 4.1 %fusion.54 = bf16[320,768]{1,0:T(8,128)(2,1)S(1)} fusion(bf16[1,3072,768]{2,1,0:T(8,128)(2,1)S(1)} %bitcast.30, f32[320,3072]{1,0:T(8,128)S(1)} %fusion.2, f32[320,3072]{1,0:T(8,128)S(1)} %get-tuple-element.7), kind=kOutput, calls=%fused_computation.40 | convolution fusion | flops 1529856000 | bytes 13074432 | tf_op jit(solution)/shard_map/rf,fd->rd/dot_general | solution.py:18
  66.3 0.3 reshape.81
  67.1 1.1 maximum_maximum_fusion
  68.2 5.2 %all-to-all-start.1 = ((bf16[64,16,256]{2,1,0:T(8,128)(2,1)}), bf16[64,16,256]{2,1,0:T(8,128)(2,1)S(1)}, u32[]{:S(2)}, u32[]{:S(2)}) async-start(bf16[64,16,256]{2,1,0:T(8,128)(2,1)} %maximum_maximum_fusion), calls=%async_computation.1 | async-start | bytes 1048576 | tf_op jit(solution)/shard_map/all_to_all | solution.py:64
  73.4 55.1 %all-to-all-done.1 = bf16[64,16,256]{2,1,0:T(8,128)(2,1)S(1)} async-done(((bf16[64,16,256]{2,1,0:T(8,128)(2,1)}), bf16[64,16,256]{2,1,0:T(8,128)(2,1)S(1)}, u32[]{:S(2)}, u32[]{:S(2)}) %all-to-all-start.1) | async-done | bytes 524320 | tf_op jit(solution)/shard_map/all_to_all | solution.py:64
  128.5 0.3 reshape.82
  128.8 0.2 fusion.74
  129.0 0.1 add.39
  129.1 0.1 multiply_reduce_fusion.1
  129.2 0.6 div.15
  129.8 1.2 convolution_convert_fusion.1
  131.0 5.5 %fusion.25 = f32[1280,768]{1,0:T(8,128)} fusion(bf16[1280,1536]{1,0:T(8,128)(2,1)} %all-gather.2.cloned.1.call-done, bf16[1,3072,768]{2,1,0:T(8,128)(2,1)} %param.14, s32[]{:T(128)S(6)} %select_n.9), kind=kOutput, calls=%fused_computation.31 | convolution fusion | flops 1509949440 | bytes 7077892 | tf_op jit(solution)/shard_map/rd,fd->rf/dot_general | solution.py:18
  136.5 11.2 %fusion.47 = bf16[1,768,768]{2,1,0:T(8,128)(2,1)} fusion(bf16[1280,1536]{1,0:T(8,128)(2,1)} %all-gather.2.cloned.1.call-done, f32[1280,768]{1,0:T(8,128)} %fusion.25, bf16[1,3072,768]{2,1,0:T(8,128)(2,1)} %param.15, s32[]{:T(128)S(6)} %select_n.9), kind=kOutput, calls=%fused_computation.39 | convolution fusion | flops 3040149504 | bytes 10223620 | tf_op jit(solution)/shard_map/rf,rd->fd/dot_general | solution.py:18
  147.7 5.8 %fusion.44 = bf16[1,768,768]{2,1,0:T(8,128)(2,1)} fusion(bf16[1280,1536]{1,0:T(8,128)(2,1)} %all-gather.2.cloned.1.call-done, f32[1280,768]{1,0:T(8,128)} %fusion.25), kind=kOutput, calls=%fused_computation.38 | convolution fusion | flops 1519386624 | bytes 7077888 | tf_op jit(solution)/shard_map/rf,rd->fd/dot_general | solution.py:18
  (22 shorter events, 0.6 us)
Async XLA Ops:
  7.2 123.8 %all-gather.2.cloned.1.call-start = ((), (), s32[]{:S(2)}) async-start(), calls=%async_computation.2 | async-start | bytes 4915200 | tf_op jit(solution)/shard_map/all_gather | solution.py:45
  55.7 4.4 %copy-start = (bf16[320,1536]{1,0:T(8,128)(2,1)S(1)}, bf16[320,1536]{1,0:T(8,128)(2,1)}, u32[]{:S(2)}) copy-start(bf16[320,1536]{1,0:T(8,128)(2,1)} %reshape.80) | copy-start | bytes 2949124
  55.7 4.4 %copy-start.2 = (bf16[1,3072,768]{2,1,0:T(8,128)(2,1)S(1)}, bf16[1,3072,768]{2,1,0:T(8,128)(2,1)}, u32[]{:S(2)}) copy-start(bf16[1,3072,768]{2,1,0:T(8,128)(2,1)} %param.15) | copy-start | bytes 14155780
  55.7 6.5 %slice-start = ((s8[4718592]{0:T(1024)(128)(4,1)}), s8[4194304]{0:T(1024)(128)(4,1)S(1)}, s32[]{:S(2)}) async-start(s8[4718592]{0:T(1024)(128)(4,1)} %bitcast.29), calls=%async_computation.3 | async-start | bytes 8388608
  60.1 2.1 %slice-start.1 = ((s8[4718592]{0:T(1024)(128)(4,1)}), s8[524288]{0:T(1024)(128)(4,1)S(1)}, s32[]{:S(2)}) async-start(s8[4718592]{0:T(1024)(128)(4,1)} %bitcast.29), calls=%async_computation.4 | async-start | bytes 1048576
  66.3 62.9 %copy-start.1 = (f32[256]{0:T(256)S(1)}, f32[256]{0:T(256)}, u32[]{:S(2)}) copy-start(f32[256]{0:T(256)} %param.10) | copy-start | bytes 3076
  68.2 60.3 %all-to-all-start.1 = ((bf16[64,16,256]{2,1,0:T(8,128)(2,1)}), bf16[64,16,256]{2,1,0:T(8,128)(2,1)S(1)}, u32[]{:S(2)}, u32[]{:S(2)}) async-start(bf16[64,16,256]{2,1,0:T(8,128)(2,1)} %maximum_maximum_fusion), calls=%async_computation.1 | async-start | bytes 1048576 | tf_op jit(solution)/shard_map/all_to_all | solution.py:64
Sparse Core Ops, SparseCore 0:
  55.7 69.5 all-gather.1

commit v2 on v1

v2 whole, which is shorter than its diff:
```python
import math
from functools import partial

import jax
import jax.numpy as jnp
from jax import lax
from jax.experimental import pallas as pl
from jax.experimental.pallas import tpu as pltpu
from jax.sharding import PartitionSpec as P

SEGS = 4
BF = jnp.bfloat16
F32 = jnp.float32
I32 = jnp.int32
MESH = pl.DeviceIdType.MESH
D = 768
FF = 3072
T = 256
E = 64
CAP = 5
W = 256
ROWS = E * CAP
BLK = 16
GRP = 16
GROUPS = E // GRP
GR = GRP * CAP
FQ = FF // 4
FC = 256


def nn(a, b):
    return lax.dot_general(a, b, (((1,), (0,)), ((), ())), preferred_element_type=F32)


def nt(a, b):
    return lax.dot_general(a, b, (((1,), (1,)), ((), ())), preferred_element_type=F32)


def gelu_pair(v):
    scale = math.sqrt(2.0 / math.pi)
    square = v * v
    t = jnp.tanh(scale * (v + 0.044715 * (square * v)))
    half = 0.5 * (1.0 + t)
    slope = half + 0.5 * v * (1.0 - t * t) * (scale * (1.0 + 0.134145 * square))
    return v * half, slope


def iota(shape, dim):
    return lax.broadcasted_iota(I32, shape, dim)


def ones_where(cond):
    return jnp.where(cond, 1.0, 0.0).astype(BF)


def kernel(
    tok_ref, up_ref, gate_ref, exp_ref, slot_ref, seg_ref, win_hbm, wout_hbm,
    dtok_ref, dgate_ref, gin_ref, gout_ref,
    win, wout, packed, near, far, rows, back, ret, acc, gate_acc, gin_acc, gout_acc, unpack,
    w_sem, near_send, far_send, ret_send, near_sem, far_sem, ret_sem, fwd_send, fwd_sem,
):
    dp = lax.axis_index("dp")
    ex = lax.axis_index("expert")
    half = dp // 2
    core = dp % 2
    zl = ex % 4
    z = 4 * half + zl

    win_copy = pltpu.make_async_copy(win_hbm.at[0], win, w_sem.at[0])
    wout_copy = pltpu.make_async_copy(wout_hbm.at[0], wout, w_sem.at[1])
    win_copy.start()
    wout_copy.start()

    barrier = pltpu.get_barrier_semaphore()

    def greet(i, carry):
        e = (ex + i) % E
        for other in range(2):
            @pl.when((i > 0) | (other != half))
            def _():
                pl.semaphore_signal(
                    barrier, inc=1, device_id={"dp": other * 2 + core, "expert": e}, device_id_type=MESH
                )
        return carry

    pl.semaphore_signal(
        barrier, inc=1, device_id={"dp": half * 2 + 1 - core, "expert": ex}, device_id_type=MESH
    )
    lax.fori_loop(0, E, greet, 0)

    seg = seg_ref[...]
    weight = jnp.zeros((1, T), F32)
    for label in range(SEGS):
        same = seg == label
        length = jnp.sum(jnp.where(same, 1.0, 0.0), axis=1, keepdims=True)
        weight = weight + jnp.where(same, T / (SEGS * jnp.maximum(length, 1.0)), 0.0)
    gate = gate_ref[...]
    slot = slot_ref[...]
    kept = slot >= 0
    relative = (exp_ref[...] - ex + E) & (E - 1)
    code = jnp.where(kept, relative * BLK + slot, -4096)
    diagonal = iota((T, T), 0) == iota((T, T), 1)

    def column(row):
        return jnp.sum(jnp.where(diagonal, jnp.broadcast_to(row, (T, T)), 0.0), axis=1, keepdims=True)

    cotangent = (up_ref[...].astype(F32) * column(weight)).astype(BF)
    d_out = (cotangent.astype(F32) * column(gate)).astype(BF)
    tokens = tok_ref[...]
    for g in range(GROUPS):
        place = iota((GRP * BLK, T), 0) + g * GRP * BLK
        x_sum = jnp.zeros((GRP * BLK, W), F32)
        c_sum = jnp.zeros((GRP * BLK, W), F32)
        for k in range(D // W):
            hot = ones_where(place - CAP * k == code)
            x_sum = x_sum + nn(hot, tokens[:, k * W : (k + 1) * W])
            c_sum = c_sum + nn(hot, d_out[:, k * W : (k + 1) * W])
        packed[g * GRP : (g + 1) * GRP, :, 0:W] = x_sum.astype(BF).reshape(GRP, BLK, W)
        packed[g * GRP : (g + 1) * GRP, :, W : 2 * W] = c_sum.astype(BF).reshape(GRP, BLK, W)
    near[0] = packed[0]

    pl.semaphore_wait(barrier, 128)

    def near_half(step):
        hop = jnp.where(step == 2, 2 + 4 * core, jnp.where(step == 3, 7, step))
        return ((z + hop) % 8) // 4

    def send_near(i, carry):
        e = (ex + i) % E
        there = near_half((e % 4 - zl + 4) % 4)
        pltpu.make_async_remote_copy(
            src_ref=packed.at[i], dst_ref=near.at[i], send_sem=near_send, recv_sem=near_sem.at[i // GRP],
            device_id={"dp": there * 2 + core, "expert": e}, device_id_type=MESH,
        ).start()
        return carry

    def send_far(i, carry):
        e = (ex + i) % E
        there = 1 - near_half((e % 4 - zl + 4) % 4)
        pltpu.make_async_remote_copy(
            src_ref=packed.at[i], dst_ref=far.at[i], send_sem=far_send, recv_sem=far_sem.at[i // GRP],
            device_id={"dp": there * 2 + core, "expert": e}, device_id_type=MESH,
        ).start()
        return carry

    lax.fori_loop(1, E, send_near, 0)
    lax.fori_loop(0, E, send_far, 0)

    spot = iota((GR, GRP * BLK), 0)
    spot = spot + 11 * ((spot * 205) >> 10)
    for k in range(D // W):
        unpack[k * GR : (k + 1) * GR, :] = ones_where(iota((GR, GRP * BLK), 1) - CAP * k == spot)

    def take(block, base):
        out = nn(unpack[...], block).astype(BF)
        for k in range(D // W):
            rows[pl.ds(base, GR), k * W : (k + 1) * W] = out[k * GR : (k + 1) * GR, 0:W]
            rows[pl.ds(base, GR), D + k * W : D + (k + 1) * W] = out[k * GR : (k + 1) * GR, W : 2 * W]

    def forward(base, index):
        return pltpu.make_async_remote_copy(
            src_ref=rows.at[pl.ds(base, GR)], dst_ref=rows.at[pl.ds(base, GR)],
            send_sem=fwd_send.at[index], recv_sem=fwd_sem.at[index],
            device_id={"dp": half * 2 + 1 - core, "expert": ex}, device_id_type=MESH,
        )

    forwards = []
    own = pl.multiple_of(core * ROWS, BLK)
    for g in range(GROUPS):
        low = 1 if g == 0 else g * GRP
        part = near.at[pl.ds(low, (g + 1) * GRP - low)]
        pltpu.make_async_copy(part, part, near_sem.at[g]).wait()
        base = pl.multiple_of(own + g * GR, BLK)
        take(near[g * GRP : (g + 1) * GRP].reshape(GRP * BLK, 2 * W), base)
        copy = forward(base, g)
        copy.start()
        forwards.append(copy)

    win_copy.wait()
    wout_copy.wait()
    acc[...] = jnp.zeros_like(acc)
    gate_acc[...] = jnp.zeros_like(gate_acc)

    def near_step(j, carry):
        units = pl.ds(pl.multiple_of(j * FC, FC), FC)
        mine = pl.ds(own, ROWS)
        pre = nt(rows[mine, 0:D], win[units, :])
        d_hidden = nt(rows[mine, D : 2 * D], wout[units, :])
        hidden, slope = gelu_pair(pre)
        gate_acc[...] += hidden.astype(BF).astype(F32) * d_hidden
        acc[...] += nn((d_hidden * slope).astype(BF), win[units, :])
        return carry

    lax.fori_loop(0, FF // FC, near_step, 0)

    spot = iota((GRP * BLK, GR), 1)
    source = (spot * 205) >> 10
    put = iota((GRP * BLK, GR), 0)
    lane = iota((GR, W), 1)
    here = iota((GR, W), 0)
    here = here - CAP * ((here * 205) >> 10)
    for g in range(GROUPS):
        sums = jnp.sum(gate_acc[g * GR : (g + 1) * GR, :], axis=1, keepdims=True)
        high = sums.astype(BF).astype(F32)
        parts = jnp.where(lane == here, high, jnp.where(lane == here + 128, sums - high, 0.0)).astype(BF)
        out = nn(ones_where(put == source * BLK + BLK - 1), parts)
        for k in range(D // W):
            hot = ones_where(put == spot + 11 * source + CAP * k)
            out = out + nn(hot, acc[g * GR : (g + 1) * GR, k * W : (k + 1) * W].astype(BF))
        back[g * GRP : (g + 1) * GRP] = out.astype(BF).reshape(GRP, BLK, W)
    ret[0] = back[0]

    def send_back(i, carry):
        e = (ex - i + E) % E
        step = (zl - e % 4 + 4) % 4
        hop = jnp.where(step == 2, 2 + 4 * core, jnp.where(step == 3, 7, step))
        there = ((z - hop + 8) % 8) // 4
        pltpu.make_async_remote_copy(
            src_ref=back.at[i], dst_ref=ret.at[i], send_sem=ret_send, recv_sem=ret_sem,
            device_id={"dp": there * 2 + core, "expert": e}, device_id_type=MESH,
        ).start()
        return carry

    lax.fori_loop(1, E, send_back, 0)

    def grads(base, count, first, last):
        def step(j, carry):
            units = pl.ds(pl.multiple_of(dp * FQ + j * FC, FC), FC)
            out = pl.ds(pl.multiple_of(j * FC, FC), FC)
            x = rows[base : base + count, 0:D]
            c = rows[base : base + count, D : 2 * D]
            hidden, slope = gelu_pair(nt(win[units, :], x))
            d_pre = (nt(wout[units, :], c) * slope).astype(BF)
            g_in = nn(d_pre, x)
            g_out = nn(hidden.astype(BF), c)
            if not first:
                g_in = g_in + gin_acc[out, :]
                g_out = g_out + gout_acc[out, :]
            if last:
                gin_ref[0, out, :] = g_in.astype(BF)
                gout_ref[0, out, :] = g_out.astype(BF)
            else:
                gin_acc[out, :] = g_in
                gout_acc[out, :] = g_out
            return carry

        lax.fori_loop(0, FQ // FC, step, 0)

    for g in range(GROUPS):
        forwards[g].wait_recv()
    grads(0, 2 * ROWS, True, False)

    def take_far(g):
        part = far.at[pl.ds(g * GRP, GRP)]
        pltpu.make_async_copy(part, part, far_sem.at[g]).wait()
        base = pl.multiple_of(2 * ROWS + 2 * g * GR + core * GR, BLK)
        take(far[g * GRP : (g + 1) * GRP].reshape(GRP * BLK, 2 * W), base)
        copy = forward(base, GROUPS + g)
        copy.start()
        forwards.append(copy)

    take_far(0)
    take_far(1)

    part = ret.at[pl.ds(1, E - 1)]
    pltpu.make_async_copy(part, part, ret_sem).wait()
    returned = ret[...].reshape(E * BLK, W)
    code_column = column(code.astype(F32)).astype(I32)
    place = iota((T, E * BLK), 1)
    for k in range(D // W):
        hot = ones_where(place == code_column + CAP * k)
        dtok_ref[:, k * W : (k + 1) * W] = nn(hot, returned).astype(BF)
    gate_place = column(jnp.where(kept, relative * BLK + BLK - 1, -4096).astype(F32)).astype(I32)
    slot_column = column(slot.astype(F32)).astype(I32)
    picked = nn(ones_where(place == gate_place), returned)
    lane = iota((T, W), 1)
    picked = jnp.where((lane == slot_column) | (lane == slot_column + 128), picked, 0.0)
    sums = jnp.sum(picked, axis=1, keepdims=True)
    sums = jnp.sum(jnp.where(diagonal, jnp.broadcast_to(sums, (T, T)), 0.0), axis=0, keepdims=True)
    dgate_ref[...] = sums / gate

    forwards[GROUPS].wait_recv()
    forwards[GROUPS + 1].wait_recv()
    grads(2 * ROWS, 256, False, False)
    take_far(2)
    take_far(3)
    forwards[GROUPS + 2].wait_recv()
    forwards[GROUPS + 3].wait_recv()
    grads(2 * ROWS + 256, 2 * ROWS - 256, False, True)

    for copy in forwards:
        copy.wait_send()
    part = packed.at[pl.ds(1, E - 1)]
    pltpu.make_async_copy(part, part, near_send).wait()
    pltpu.make_async_copy(packed, packed, far_send).wait()
    part = back.at[pl.ds(1, E - 1)]
    pltpu.make_async_copy(part, part, ret_send).wait()


def body(tokens, upstream, gate_prob, expert_id, slot_index, segment_id, weight_in, weight_out):
    vmem = pl.BlockSpec(memory_space=pltpu.VMEM)
    hbm = pl.BlockSpec(memory_space=pl.ANY)
    dma = pltpu.SemaphoreType.DMA
    d_tokens, d_gate, grad_in, grad_out = pl.pallas_call(
        kernel,
        out_shape=(
            jax.ShapeDtypeStruct((T, D), BF),
            jax.ShapeDtypeStruct((1, T), F32),
            jax.ShapeDtypeStruct((1, FQ, D), BF),
            jax.ShapeDtypeStruct((1, FQ, D), BF),
        ),
        in_specs=[vmem] * 6 + [hbm] * 2,
        out_specs=(vmem, vmem, vmem, vmem),
        scratch_shapes=[
            pltpu.VMEM((FF, D), BF),
            pltpu.VMEM((FF, D), BF),
            pltpu.VMEM((E, BLK, 2 * W), BF),
            pltpu.VMEM((E, BLK, 2 * W), BF),
            pltpu.VMEM((E, BLK, 2 * W), BF),
            pltpu.VMEM((4 * ROWS, 2 * D), BF),
            pltpu.VMEM((E, BLK, W), BF),
            pltpu.VMEM((E, BLK, W), BF),
            pltpu.VMEM((ROWS, D), F32),
            pltpu.VMEM((ROWS, FC), F32),
            pltpu.VMEM((FQ, D), F32),
            pltpu.VMEM((FQ, D), F32),
            pltpu.VMEM((D // W * GR, GRP * BLK), BF),
            dma((2,)),
            dma,
            dma,
            dma,
            dma((GROUPS,)),
            dma((GROUPS,)),
            dma,
            dma((2 * GROUPS,)),
            dma((2 * GROUPS,)),
        ],
        compiler_params=pltpu.CompilerParams(
            collective_id=0, has_side_effects=True, vmem_limit_bytes=52 * 2**20
        ),
    )(
        tokens,
        upstream,
        gate_prob.reshape(1, T),
        expert_id.reshape(1, T),
        slot_index.reshape(1, T),
        segment_id,
        weight_in,
        weight_out,
    )
    return d_tokens, d_gate.reshape(T), grad_in, grad_out


def solution(mesh):
    in_specs = (
        P(("dp", "expert"), None),
        P(("dp", "expert"), None),
        P(("dp", "expert")),
        P(("dp", "expert")),
        P(("dp", "expert")),
        P(("dp", "expert"), None),
        P("expert", None, None),
        P("expert", None, None),
    )
    out_specs = (
        P(("dp", "expert"), None),
        P(("dp", "expert")),
        P("expert", "dp", None),
        P("expert", "dp", None),
    )
    return jax.shard_map(body, mesh=mesh, in_specs=in_specs, out_specs=out_specs, check_vma=False)
```

time: 161 us -> 89.1 us (0.55)
  Pallas kernels: 0 us -> 78.7 us
  waiting for transfers between devices: 55.1 us -> 0 us
  blocking collectives: 40.7 us -> 0 us
  matrix products: 35.7 us -> 0 us
  between operations: 14.2 us -> 0.66 us
  local copies, waits for them, and re-layouts: 4.04 us -> 9.48 us
  other arithmetic: 5.41 us -> 0 us
  starting transfers between devices: 5.24 us -> 0 us
    pallas_call x0 -> x1, Pallas kernels: none -> 78.7 us  [body(): pl.pallas_call(kernel, out_shape=(jax.ShapeDtypeStruct((T, D), BF), jax.S...]
    all_to_all x1 -> x0, waiting for transfers between devices: 55.1 us -> none  [body(): lax.all_to_all(back, 'expert', split_axis=0, concat_axis=0, tiled=True)]
    all_to_all x1 -> x0, blocking collectives: 40.7 us -> none  [body(): lax.all_to_all(sent, 'expert', split_axis=0, concat_axis=0, tiled=True)]
    dot_general x8 -> x0, matrix products: 35.7 us -> none  [mm(): return jnp.einsum(spec, a, b, preferred_element_type=F32)]
    unnamed x10 -> x18, local copies, waits for them, and re-layouts: 0.03 us -> 9.48 us
    all_to_all x1 -> x0, starting transfers between devices: 5.2 us -> none  [body(): lax.all_to_all(back, 'expert', split_axis=0, concat_axis=0, tiled=True)]
    reshape x4 -> x0, local copies, waits for them, and re-layouts: 3.36 us -> none  [the longest x1 1.85 us: body(): rows = got.reshape(slots_all, 2 * width)]
    reduce_sum x3 -> x0, other arithmetic: 1.69 us -> none  [the longest x1 0.8 us: body(): counts = jnp.sum(member, axis=0)]
  transfers between devices with their start and end apart: 2 -> 0, of which waited for: 1 -> 0; matrix products, arithmetic and copies ran while one was open for 9% -> 0% of each run, Pallas kernels for 0% -> 0%
where the time goes in v2:
time: 89.1 us; the launch traced here: 88.9 us
  Pallas kernels  78.7 us (88%)
  local copies, waits for them, and re-layouts  9.48 us (11%)
    pallas_call x1, Pallas kernels, body(): pl.pallas_call(kernel, out_shape=(jax.ShapeDtypeStruct((T, D), BF), jax.S...  78.7 us
    unnamed x18, local copies, waits for them, and re-layouts  9.48 us

profile of v2, /device:TPU:1, one launch (start us, length us, event | category | flops | bytes accessed | tf_op | source)
XLA Modules:
  0.0 88.9 jit_solution(2910609819977340053)
XLA Ops:
  0.6 0.0 copy-start
  0.6 1.0 %copy-done = bf16[256,768]{1,0:T(8,128)(2,1)S(1)} copy-done((bf16[256,768]{1,0:T(8,128)(2,1)S(1)}, bf16[256,768]{1,0:T(8,128)(2,1)}, u32[]{:S(2)}) %copy-start) | copy-done | bytes 393240
  1.6 0.0 copy-start.1
  1.6 1.0 %copy-done.1 = bf16[256,768]{1,0:T(8,128)(2,1)S(1)} copy-done((bf16[256,768]{1,0:T(8,128)(2,1)S(1)}, bf16[256,768]{1,0:T(8,128)(2,1)}, u32[]{:S(2)}) %copy-start.1) | copy-done | bytes 393240
  2.6 0.0 copy-start.2
  2.6 0.7 copy-done.2
  3.3 0.0 copy-start.3
  3.3 0.7 copy-done.3
  4.0 0.0 copy-start.4
  4.0 0.7 copy-done.4
  4.7 0.0 copy-start.5
  4.7 0.7 copy-done.5
  5.3 78.7 %shard_map.111 = (bf16[256,768]{1,0:T(8,128)(2,1)S(1)}, f32[1,256]{1,0:T(1,128)S(1)}, bf16[1,768,768]{2,1,0:T(8,128)(2,1)}, bf16[1,768,768]{2,1,0:T(8,128)(2,1)}) custom-call(bf16[256,768]{1,0:T(8,128)(2,1)S(1)} %copy-done, bf16[256,768]{1,0:T(8,128)(2,1)S(1)} %copy-done.1, f32[1,256]{1,0:T(1,128)S(1)} %bitcast.4, s32[1,256]{1,0:T(1,128)S(1)} %bitcast.5, ...), custom_call_target="tpu_custom_call" | custom-call | tf_op jit(solution)/shard_map/pallas_call | solution.py:304
  84.1 0.7 copy.16
  84.8 0.6 copy.17
  85.4 0.0 copy-start.6
  85.4 2.5 %copy.18 = bf16[1,768,768]{2,1,0:T(8,128)(2,1)} copy(bf16[1,768,768]{2,1,0:T(8,128)(2,1)} %get-tuple-element.18) | data formatting | bytes 2359296
  87.9 0.0 copy-done.6
  87.9 1.0 %copy.19 = bf16[1,768,768]{2,1,0:T(8,128)(2,1)} copy(bf16[1,768,768]{2,1,0:T(8,128)(2,1)S(1)} %copy-done.6) | data formatting | bytes 2359296
Async XLA Ops:
  0.6 1.0 %copy-start = (bf16[256,768]{1,0:T(8,128)(2,1)S(1)}, bf16[256,768]{1,0:T(8,128)(2,1)}, u32[]{:S(2)}) copy-start(bf16[256,768]{1,0:T(8,128)(2,1)} %tok_ref.1) | copy-start | bytes 1179652
  1.6 1.0 %copy-start.1 = (bf16[256,768]{1,0:T(8,128)(2,1)S(1)}, bf16[256,768]{1,0:T(8,128)(2,1)}, u32[]{:S(2)}) copy-start(bf16[256,768]{1,0:T(8,128)(2,1)} %up_ref.1) | copy-start | bytes 1179652
  2.6 0.7 copy-start.2
  3.3 0.7 copy-start.3
  4.0 0.7 copy-start.4
  4.7 0.7 copy-start.5
  85.4 2.5 %copy-start.6 = (bf16[1,768,768]{2,1,0:T(8,128)(2,1)S(1)}, bf16[1,768,768]{2,1,0:T(8,128)(2,1)}, u32[]{:S(2)}) copy-start(bf16[1,768,768]{2,1,0:T(8,128)(2,1)} %get-tuple-element.19) | copy-start | bytes 3538948

commit v3 on v2

--- a/solution.py
+++ b/solution.py
@@ -26,6 +26,9 @@
 GR = GRP * CAP
 FQ = FF // 4
 FC = 256
+LIMIT = 60
+FIRST = 28
+PACE = 3
 
 
 def nn(a, b):
@@ -54,10 +57,10 @@
 
 
 def kernel(
-    tok_ref, up_ref, gate_ref, exp_ref, slot_ref, seg_ref, win_hbm, wout_hbm,
+    tok_hbm, up_hbm, gate_hbm, exp_hbm, slot_hbm, seg_hbm, win_hbm, wout_hbm,
     dtok_ref, dgate_ref, gin_ref, gout_ref,
-    win, wout, packed, near, far, rows, back, ret, acc, gate_acc, gin_acc, gout_acc, unpack,
-    w_sem, near_send, far_send, ret_send, near_sem, far_sem, ret_sem, fwd_send, fwd_sem,
+    tok_ref, up_ref, gate_ref, exp_ref, slot_ref, seg_ref, win, wout, packed, near, far, rows, back, ret, acc, gate_acc, gin_acc, gout_acc, unpack,
+    in_sem, w_sem, ready, near_send, far_send, ret_send, near_sem, far_sem, ret_sem, fwd_send, fwd_sem,
 ):
     dp = lax.axis_index("dp")
     ex = lax.axis_index("expert")
@@ -66,27 +69,42 @@
     zl = ex % 4
     z = 4 * half + zl
 
+    x, y = ex // 16, ex // 4 % 4
+    loads = [
+        pltpu.make_async_copy(source, target, in_sem.at[index])
+        for index, (source, target) in enumerate(
+            (
+                (up_hbm, up_ref),
+                (tok_hbm, tok_ref),
+                (seg_hbm, seg_ref),
+                (gate_hbm, gate_ref),
+                (exp_hbm, exp_ref),
+                (slot_hbm, slot_ref),
+            )
+        )
+    ]
+    for load in loads:
+        load.start()
+
+    def signal(semaphore, group, expert):
+        pl.semaphore_signal(semaphore, inc=1, device_id={"dp": group, "expert": expert}, device_id_type=MESH)
+
+    def signal_ring(semaphore):
+        for hop in range(1, 8):
+            there = (z + hop) % 8
+            signal(semaphore, there // 4 * 2 + core, ex - zl + there % 4)
+
+    barrier = pltpu.get_barrier_semaphore()
+    signal(barrier, half * 2 + 1 - core, ex)
+    for hop in range(1, 16):
+        signal(barrier, dp, (x + hop // 4) % 4 * 16 + (y + hop % 4) % 4 * 4 + zl)
+    signal_ring(barrier)
+    for load in loads:
+        load.wait()
     win_copy = pltpu.make_async_copy(win_hbm.at[0], win, w_sem.at[0])
     wout_copy = pltpu.make_async_copy(wout_hbm.at[0], wout, w_sem.at[1])
     win_copy.start()
     wout_copy.start()
-
-    barrier = pltpu.get_barrier_semaphore()
-
-    def greet(i, carry):
-        e = (ex + i) % E
-        for other in range(2):
-            @pl.when((i > 0) | (other != half))
-            def _():
-                pl.semaphore_signal(
-                    barrier, inc=1, device_id={"dp": other * 2 + core, "expert": e}, device_id_type=MESH
-                )
-        return carry
-
-    pl.semaphore_signal(
-        barrier, inc=1, device_id={"dp": half * 2 + 1 - core, "expert": ex}, device_id_type=MESH
-    )
-    lax.fori_loop(0, E, greet, 0)
 
     seg = seg_ref[...]
     weight = jnp.zeros((1, T), F32)
@@ -107,6 +125,31 @@
     cotangent = (up_ref[...].astype(F32) * column(weight)).astype(BF)
     d_out = (cotangent.astype(F32) * column(gate)).astype(BF)
     tokens = tok_ref[...]
+    pl.semaphore_wait(barrier, 23)
+    signal_ring(ready)
+
+    def near_half(step):
+        hop = jnp.where(step == 2, 2 + 4 * core, jnp.where(step == 3, 7, step))
+        return ((z + hop) % 8) // 4
+
+    def send_near(i, carry):
+        e = (ex + i) % E
+        there = near_half((e % 4 - zl + 4) % 4)
+        pltpu.make_async_remote_copy(
+            src_ref=packed.at[i], dst_ref=near.at[i], send_sem=near_send, recv_sem=near_sem.at[i // GRP],
+            device_id={"dp": there * 2 + core, "expert": e}, device_id_type=MESH,
+        ).start()
+        return carry
+
+    def send_far(i, carry):
+        e = (ex + i) % E
+        there = 1 - near_half((e % 4 - zl + 4) % 4)
+        pltpu.make_async_remote_copy(
+            src_ref=packed.at[i], dst_ref=far.at[i], send_sem=far_send, recv_sem=far_sem.at[i // GRP],
+            device_id={"dp": there * 2 + core, "expert": e}, device_id_type=MESH,
+        ).start()
+        return carry
+
     for g in range(GROUPS):
         place = iota((GRP * BLK, T), 0) + g * GRP * BLK
         x_sum = jnp.zeros((GRP * BLK, W), F32)
@@ -117,34 +160,11 @@
             c_sum = c_sum + nn(hot, d_out[:, k * W : (k + 1) * W])
         packed[g * GRP : (g + 1) * GRP, :, 0:W] = x_sum.astype(BF).reshape(GRP, BLK, W)
         packed[g * GRP : (g + 1) * GRP, :, W : 2 * W] = c_sum.astype(BF).reshape(GRP, BLK, W)
-    near[0] = packed[0]
-
-    pl.semaphore_wait(barrier, 128)
-
-    def near_half(step):
-        hop = jnp.where(step == 2, 2 + 4 * core, jnp.where(step == 3, 7, step))
-        return ((z + hop) % 8) // 4
-
-    def send_near(i, carry):
-        e = (ex + i) % E
-        there = near_half((e % 4 - zl + 4) % 4)
-        pltpu.make_async_remote_copy(
-            src_ref=packed.at[i], dst_ref=near.at[i], send_sem=near_send, recv_sem=near_sem.at[i // GRP],
-            device_id={"dp": there * 2 + core, "expert": e}, device_id_type=MESH,
-        ).start()
-        return carry
-
-    def send_far(i, carry):
-        e = (ex + i) % E
-        there = 1 - near_half((e % 4 - zl + 4) % 4)
-        pltpu.make_async_remote_copy(
-            src_ref=packed.at[i], dst_ref=far.at[i], send_sem=far_send, recv_sem=far_sem.at[i // GRP],
-            device_id={"dp": there * 2 + core, "expert": e}, device_id_type=MESH,
-        ).start()
-        return carry
-
-    lax.fori_loop(1, E, send_near, 0)
-    lax.fori_loop(0, E, send_far, 0)
+        if g == 0:
+            near[0] = packed[0]
+            pl.semaphore_wait(ready, 7)
+        lax.fori_loop(max(1, g * GRP), (g + 1) * GRP, send_near, 0)
+    lax.fori_loop(0, FIRST, send_far, 0)
 
     spot = iota((GR, GRP * BLK), 0)
     spot = spot + 11 * ((spot * 205) >> 10)
@@ -182,6 +202,8 @@
     gate_acc[...] = jnp.zeros_like(gate_acc)
 
     def near_step(j, carry):
+        for extra in range(PACE):
+            send_far(FIRST + PACE * j + extra, 0)
         units = pl.ds(pl.multiple_of(j * FC, FC), FC)
         mine = pl.ds(own, ROWS)
         pre = nt(rows[mine, 0:D], win[units, :])
@@ -226,7 +248,7 @@
     def grads(base, count, first, last):
         def step(j, carry):
             units = pl.ds(pl.multiple_of(dp * FQ + j * FC, FC), FC)
-            out = pl.ds(pl.multiple_of(j * FC, FC), FC)
+            out = pl.ds(j * FC if last else pl.multiple_of(j * FC, FC), FC)
             x = rows[base : base + count, 0:D]
             c = rows[base : base + count, D : 2 * D]
             hidden, slope = gelu_pair(nt(win[units, :], x))
@@ -244,7 +266,11 @@
                 gout_acc[out, :] = g_out
             return carry
 
-        lax.fori_loop(0, FQ // FC, step, 0)
+        if last:
+            for j in range(FQ // FC):
+                step(j, 0)
+        else:
+            lax.fori_loop(0, FQ // FC, step, 0)
 
     for g in range(GROUPS):
         forwards[g].wait_recv()
@@ -261,6 +287,16 @@
 
     take_far(0)
     take_far(1)
+
+    forwards[GROUPS].wait_recv()
+    forwards[GROUPS + 1].wait_recv()
+    grads(2 * ROWS, 4 * GR, False, False)
+    take_far(2)
+    forwards[GROUPS + 2].wait_recv()
+    grads(2 * ROWS + 4 * GR, 2 * GR, False, False)
+    take_far(3)
+    forwards[GROUPS + 3].wait_recv()
+    grads(2 * ROWS + 6 * GR, 2 * GR, False, True)
 
     part = ret.at[pl.ds(1, E - 1)]
     pltpu.make_async_copy(part, part, ret_sem).wait()
@@ -279,15 +315,6 @@
     sums = jnp.sum(jnp.where(diagonal, jnp.broadcast_to(sums, (T, T)), 0.0), axis=0, keepdims=True)
     dgate_ref[...] = sums / gate
 
-    forwards[GROUPS].wait_recv()
-    forwards[GROUPS + 1].wait_recv()
-    grads(2 * ROWS, 256, False, False)
-    take_far(2)
-    take_far(3)
-    forwards[GROUPS + 2].wait_recv()
-    forwards[GROUPS + 3].wait_recv()
-    grads(2 * ROWS + 256, 2 * ROWS - 256, False, True)
-
     for copy in forwards:
         copy.wait_send()
     part = packed.at[pl.ds(1, E - 1)]
@@ -295,6 +322,20 @@
     pltpu.make_async_copy(packed, packed, far_send).wait()
     part = back.at[pl.ds(1, E - 1)]
     pltpu.make_async_copy(part, part, ret_send).wait()
+
+
+def deliver(*refs):
+    sources, targets, stage = refs[:4], refs[4:8], refs[8:12]
+    inward, outward = refs[12:]
+    loads = [pltpu.make_async_copy(sources[i], stage[i], inward.at[i]) for i in range(4)]
+    stores = [pltpu.make_async_copy(stage[i], targets[i], outward.at[i]) for i in range(4)]
+    for load in loads:
+        load.start()
+    for load, store in zip(loads, stores):
+        load.wait()
+        store.start()
+    for store in stores:
+        store.wait()
 
 
 def body(tokens, upstream, gate_prob, expert_id, slot_index, segment_id, weight_in, weight_out):
@@ -309,9 +350,15 @@
             jax.ShapeDtypeStruct((1, FQ, D), BF),
             jax.ShapeDtypeStruct((1, FQ, D), BF),
         ),
-        in_specs=[vmem] * 6 + [hbm] * 2,
+        in_specs=[hbm] * 8,
         out_specs=(vmem, vmem, vmem, vmem),
         scratch_shapes=[
+            pltpu.VMEM((T, D), BF),
+            pltpu.VMEM((T, D), BF),
+            pltpu.VMEM((1, T), F32),
+            pltpu.VMEM((1, T), I32),
+            pltpu.VMEM((1, T), I32),
+            pltpu.VMEM((1, T), I32),
             pltpu.VMEM((FF, D), BF),
             pltpu.VMEM((FF, D), BF),
             pltpu.VMEM((E, BLK, 2 * W), BF),
@@ -325,7 +372,9 @@
             pltpu.VMEM((FQ, D), F32),
             pltpu.VMEM((FQ, D), F32),
             pltpu.VMEM((D // W * GR, GRP * BLK), BF),
+            dma((6,)),
             dma((2,)),
+            pltpu.SemaphoreType.REGULAR,
             dma,
             dma,
             dma,
@@ -336,7 +385,7 @@
             dma((2 * GROUPS,)),
         ],
         compiler_params=pltpu.CompilerParams(
-            collective_id=0, has_side_effects=True, vmem_limit_bytes=52 * 2**20
+            collective_id=0, has_side_effects=True, vmem_limit_bytes=LIMIT * 2**20
         ),
     )(
         tokens,
@@ -348,6 +397,14 @@
         weight_in,
         weight_out,
     )
+    results = (d_tokens, d_gate, grad_in, grad_out)
+    d_tokens, d_gate, grad_in, grad_out = pl.pallas_call(
+        deliver,
+        out_shape=tuple(jax.ShapeDtypeStruct(r.shape, r.dtype) for r in results),
+        in_specs=[hbm] * 4,
+        out_specs=(hbm,) * 4,
+        scratch_shapes=[pltpu.VMEM(r.shape, r.dtype) for r in results] + [dma((4,)), dma((4,))],
+    )(*results)
     return d_tokens, d_gate.reshape(T), grad_in, grad_out
 
 

time: 89.1 us -> 75.1 us (0.84)
  local copies, waits for them, and re-layouts: 9.48 us -> 0 us
  Pallas kernels: 78.7 us -> 74.3 us
    unnamed x18 -> x0, local copies, waits for them, and re-layouts: 9.48 us -> none
    pallas_call x1, Pallas kernels: 78.7 us -> 71.5 us  [body(): pl.pallas_call(kernel, out_shape=(jax.ShapeDtypeStruct((T, D), BF), jax.S...]
    pallas_call x0 -> x1, Pallas kernels: none -> 2.87 us  [body(): pl.pallas_call(deliver, out_shape=tuple((jax.ShapeDtypeStruct(r.shape, r....]
where the time goes in v3:
time: 75.1 us; the launch traced here: 75 us
  Pallas kernels  74.3 us (99%)
    pallas_call x1, Pallas kernels, body(): pl.pallas_call(kernel, out_shape=(jax.ShapeDtypeStruct((T, D), BF), jax.S...  71.5 us
    pallas_call x1, Pallas kernels, body(): pl.pallas_call(deliver, out_shape=tuple((jax.ShapeDtypeStruct(r.shape, r....  2.87 us

profile of v3, /device:TPU:1, one launch (start us, length us, event | category | flops | bytes accessed | tf_op | source)
XLA Modules:
  0.0 75.0 jit_solution(5146352152126395570)
XLA Ops:
  0.6 71.5 %shard_map.111 = (bf16[256,768]{1,0:T(8,128)(2,1)}, f32[1,256]{1,0:T(1,128)}, bf16[1,768,768]{2,1,0:T(8,128)(2,1)}, bf16[1,768,768]{2,1,0:T(8,128)(2,1)}) custom-call(bf16[256,768]{1,0:T(8,128)(2,1)} %tok_hbm.1, bf16[256,768]{1,0:T(8,128)(2,1)} %up_hbm.1, f32[1,256]{1,0:T(1,128)} %bitcast.4, s32[1,256]{1,0:T(1,128)} %bitcast.5, s32[1,256]{1,0:T(1,128)} %bitcast.6, ...), custom_call_target="tpu_custom_call" | custom-call | tf_op jit(solution)/shard_map/pallas_call | solution.py:345
  72.1 2.9 %shard_map.112 = (bf16[256,768]{1,0:T(8,128)(2,1)}, f32[1,256]{1,0:T(1,128)}, bf16[1,768,768]{2,1,0:T(8,128)(2,1)}, bf16[1,768,768]{2,1,0:T(8,128)(2,1)}) custom-call(bf16[256,768]{1,0:T(8,128)(2,1)} %get-tuple-element.12.refs_0_, f32[1,256]{1,0:T(1,128)} %get-tuple-element.13.refs_1_, bf16[1,768,768]{2,1,0:T(8,128)(2,1)} %get-tuple-element.14.refs_2_, ...), custom_call_target="tpu_custom_call" | custom-call | tf_op jit(solution)/shard_map/pallas_call | solution.py:401

commit v4 on v3

--- a/solution.py
+++ b/solution.py
@@ -56,11 +56,16 @@
     return jnp.where(cond, 1.0, 0.0).astype(BF)
 
 
+def column(row):
+    diagonal = iota((T, T), 0) == iota((T, T), 1)
+    return jnp.sum(jnp.where(diagonal, jnp.broadcast_to(row, (T, T)), 0.0), axis=1, keepdims=True)
+
+
 def kernel(
     tok_hbm, up_hbm, gate_hbm, exp_hbm, slot_hbm, seg_hbm, win_hbm, wout_hbm,
-    dtok_ref, dgate_ref, gin_ref, gout_ref,
-    tok_ref, up_ref, gate_ref, exp_ref, slot_ref, seg_ref, win, wout, packed, near, far, rows, back, ret, acc, gate_acc, gin_acc, gout_acc, unpack,
-    in_sem, w_sem, ready, near_send, far_send, ret_send, near_sem, far_sem, ret_sem, fwd_send, fwd_sem,
+    ret, gin_out, gout_out,
+    tok_ref, up_ref, gate_ref, exp_ref, slot_ref, seg_ref, win, wout, packed, near, far, rows, back, gin_ref, gout_ref, acc, gate_acc, gin_acc, gout_acc, unpack,
+    in_sem, w_sem, ready, near_send, far_send, ret_send, near_sem, far_sem, ret_sem, fwd_send, fwd_sem, out_sem,
 ):
     dp = lax.axis_index("dp")
     ex = lax.axis_index("expert")
@@ -117,11 +122,6 @@
     kept = slot >= 0
     relative = (exp_ref[...] - ex + E) & (E - 1)
     code = jnp.where(kept, relative * BLK + slot, -4096)
-    diagonal = iota((T, T), 0) == iota((T, T), 1)
-
-    def column(row):
-        return jnp.sum(jnp.where(diagonal, jnp.broadcast_to(row, (T, T)), 0.0), axis=1, keepdims=True)
-
     cotangent = (up_ref[...].astype(F32) * column(weight)).astype(BF)
     d_out = (cotangent.astype(F32) * column(gate)).astype(BF)
     tokens = tok_ref[...]
@@ -230,7 +230,8 @@
             hot = ones_where(put == spot + 11 * source + CAP * k)
             out = out + nn(hot, acc[g * GR : (g + 1) * GR, k * W : (k + 1) * W].astype(BF))
         back[g * GRP : (g + 1) * GRP] = out.astype(BF).reshape(GRP, BLK, W)
-    ret[0] = back[0]
+    kept_block = pltpu.make_async_copy(back.at[0], ret.at[0], out_sem.at[2 * FQ // FC])
+    kept_block.start()
 
     def send_back(i, carry):
         e = (ex - i + E) % E
@@ -244,6 +245,8 @@
         return carry
 
     lax.fori_loop(1, E, send_back, 0)
+
+    stores = [kept_block]
 
     def grads(base, count, first, last):
         def step(j, carry):
@@ -259,8 +262,14 @@
                 g_in = g_in + gin_acc[out, :]
                 g_out = g_out + gout_acc[out, :]
             if last:
-                gin_ref[0, out, :] = g_in.astype(BF)
-                gout_ref[0, out, :] = g_out.astype(BF)
+                gin_ref[out, :] = g_in.astype(BF)
+                gout_ref[out, :] = g_out.astype(BF)
+                for index, (source, target) in enumerate(((gin_ref, gin_out), (gout_ref, gout_out))):
+                    copy = pltpu.make_async_copy(
+                        source.at[out], target.at[0, out], out_sem.at[2 * j + index]
+                    )
+                    copy.start()
+                    stores.append(copy)
             else:
                 gin_acc[out, :] = g_in
                 gout_acc[out, :] = g_out
@@ -300,21 +309,8 @@
 
     part = ret.at[pl.ds(1, E - 1)]
     pltpu.make_async_copy(part, part, ret_sem).wait()
-    returned = ret[...].reshape(E * BLK, W)
-    code_column = column(code.astype(F32)).astype(I32)
-    place = iota((T, E * BLK), 1)
-    for k in range(D // W):
-        hot = ones_where(place == code_column + CAP * k)
-        dtok_ref[:, k * W : (k + 1) * W] = nn(hot, returned).astype(BF)
-    gate_place = column(jnp.where(kept, relative * BLK + BLK - 1, -4096).astype(F32)).astype(I32)
-    slot_column = column(slot.astype(F32)).astype(I32)
-    picked = nn(ones_where(place == gate_place), returned)
-    lane = iota((T, W), 1)
-    picked = jnp.where((lane == slot_column) | (lane == slot_column + 128), picked, 0.0)
-    sums = jnp.sum(picked, axis=1, keepdims=True)
-    sums = jnp.sum(jnp.where(diagonal, jnp.broadcast_to(sums, (T, T)), 0.0), axis=0, keepdims=True)
-    dgate_ref[...] = sums / gate
-
+    for copy in stores:
+        copy.wait()
     for copy in forwards:
         copy.wait_send()
     part = packed.at[pl.ds(1, E - 1)]
@@ -324,34 +320,62 @@
     pltpu.make_async_copy(part, part, ret_send).wait()
 
 
-def deliver(*refs):
-    sources, targets, stage = refs[:4], refs[4:8], refs[8:12]
-    inward, outward = refs[12:]
-    loads = [pltpu.make_async_copy(sources[i], stage[i], inward.at[i]) for i in range(4)]
-    stores = [pltpu.make_async_copy(stage[i], targets[i], outward.at[i]) for i in range(4)]
+def deliver(
+    ret_hbm, gin_hbm, gout_hbm, gate_hbm, exp_hbm, slot_hbm,
+    dtok_out, dgate_out, gin_out, gout_out,
+    ret, gin, gout, gate_ref, exp_ref, slot_ref, dtok, dgate, in_sem, out_sem,
+):
+    ex = lax.axis_index("expert")
+    pairs = (
+        (exp_hbm, exp_ref), (slot_hbm, slot_ref), (gate_hbm, gate_ref),
+        (ret_hbm, ret), (gin_hbm, gin), (gout_hbm, gout),
+    )
+    loads = [pltpu.make_async_copy(a, b, in_sem.at[i]) for i, (a, b) in enumerate(pairs)]
+    pairs = ((gin, gin_out), (gout, gout_out), (dtok, dtok_out), (dgate, dgate_out))
+    stores = [pltpu.make_async_copy(a, b, out_sem.at[i]) for i, (a, b) in enumerate(pairs)]
     for load in loads:
         load.start()
-    for load, store in zip(loads, stores):
+    for load in loads[:3]:
+        load.wait()
+    slot = slot_ref[...]
+    kept = slot >= 0
+    relative = (exp_ref[...] - ex + E) & (E - 1)
+    code = column(jnp.where(kept, relative * BLK, -4096).astype(F32)).astype(I32)
+    slot_column = column(slot.astype(F32)).astype(I32)
+    place = iota((T, E * BLK), 1) - code
+    hots = [ones_where(place == slot_column + CAP * k) for k in range(D // W)]
+    gate_hot = ones_where(place == BLK - 1)
+    for load, store in zip(loads[4:], stores[:2]):
         load.wait()
         store.start()
+    loads[3].wait()
+    returned = ret[...].reshape(E * BLK, W)
+    for k in range(D // W):
+        dtok[:, k * W : (k + 1) * W] = nn(hots[k], returned).astype(BF)
+    stores[2].start()
+    picked = nn(gate_hot, returned)
+    lane = iota((T, W), 1)
+    picked = jnp.where((lane == slot_column) | (lane == slot_column + 128), picked, 0.0)
+    sums = jnp.sum(picked, axis=1, keepdims=True)
+    diagonal = iota((T, T), 0) == iota((T, T), 1)
+    sums = jnp.sum(jnp.where(diagonal, jnp.broadcast_to(sums, (T, T)), 0.0), axis=0, keepdims=True)
+    dgate[...] = sums / gate_ref[...]
+    stores[3].start()
     for store in stores:
         store.wait()
 
 
 def body(tokens, upstream, gate_prob, expert_id, slot_index, segment_id, weight_in, weight_out):
-    vmem = pl.BlockSpec(memory_space=pltpu.VMEM)
     hbm = pl.BlockSpec(memory_space=pl.ANY)
     dma = pltpu.SemaphoreType.DMA
-    d_tokens, d_gate, grad_in, grad_out = pl.pallas_call(
+    shape = jax.ShapeDtypeStruct
+    gate_row, expert_row, slot_row = (v.reshape(1, T) for v in (gate_prob, expert_id, slot_index))
+    gradient = shape((1, FQ, D), BF)
+    returned, grad_in, grad_out = pl.pallas_call(
         kernel,
-        out_shape=(
-            jax.ShapeDtypeStruct((T, D), BF),
-            jax.ShapeDtypeStruct((1, T), F32),
-            jax.ShapeDtypeStruct((1, FQ, D), BF),
-            jax.ShapeDtypeStruct((1, FQ, D), BF),
-        ),
+        out_shape=(shape((E, BLK, W), BF), gradient, gradient),
         in_specs=[hbm] * 8,
-        out_specs=(vmem, vmem, vmem, vmem),
+        out_specs=(hbm,) * 3,
         scratch_shapes=[
             pltpu.VMEM((T, D), BF),
             pltpu.VMEM((T, D), BF),
@@ -366,7 +390,8 @@
             pltpu.VMEM((E, BLK, 2 * W), BF),
             pltpu.VMEM((4 * ROWS, 2 * D), BF),
             pltpu.VMEM((E, BLK, W), BF),
-            pltpu.VMEM((E, BLK, W), BF),
+            pltpu.VMEM((FQ, D), BF),
+            pltpu.VMEM((FQ, D), BF),
             pltpu.VMEM((ROWS, D), F32),
             pltpu.VMEM((ROWS, FC), F32),
             pltpu.VMEM((FQ, D), F32),
@@ -383,28 +408,31 @@
             dma,
             dma((2 * GROUPS,)),
             dma((2 * GROUPS,)),
+            dma((2 * FQ // FC + 1,)),
         ],
         compiler_params=pltpu.CompilerParams(
             collective_id=0, has_side_effects=True, vmem_limit_bytes=LIMIT * 2**20
         ),
-    )(
-        tokens,
-        upstream,
-        gate_prob.reshape(1, T),
-        expert_id.reshape(1, T),
-        slot_index.reshape(1, T),
-        segment_id,
-        weight_in,
-        weight_out,
-    )
-    results = (d_tokens, d_gate, grad_in, grad_out)
+    )(tokens, upstream, gate_row, expert_row, slot_row, segment_id, weight_in, weight_out)
     d_tokens, d_gate, grad_in, grad_out = pl.pallas_call(
         deliver,
-        out_shape=tuple(jax.ShapeDtypeStruct(r.shape, r.dtype) for r in results),
-        in_specs=[hbm] * 4,
+        out_shape=(shape((T, D), BF), shape((1, T), F32), gradient, gradient),
+        in_specs=[hbm] * 6,
         out_specs=(hbm,) * 4,
-        scratch_shapes=[pltpu.VMEM(r.shape, r.dtype) for r in results] + [dma((4,)), dma((4,))],
-    )(*results)
+        scratch_shapes=[
+            pltpu.VMEM((E, BLK, W), BF),
+            pltpu.VMEM((1, FQ, D), BF),
+            pltpu.VMEM((1, FQ, D), BF),
+            pltpu.VMEM((1, T), F32),
+            pltpu.VMEM((1, T), I32),
+            pltpu.VMEM((1, T), I32),
+            pltpu.VMEM((T, D), BF),
+            pltpu.VMEM((1, T), F32),
+            dma((6,)),
+            dma((4,)),
+        ],
+        compiler_params=pltpu.CompilerParams(vmem_limit_bytes=LIMIT * 2**20),
+    )(returned, grad_in, grad_out, gate_row, expert_row, slot_row)
     return d_tokens, d_gate.reshape(T), grad_in, grad_out
 
 

time: 75.1 us -> 73.4 us (0.977)
  Pallas kernels: 74.3 us -> 72.6 us
    pallas_call x2, Pallas kernels: 74.3 us -> 72.6 us  [the longest x1 69.2 us: body(): pl.pallas_call(kernel, out_shape=(shape((E, BLK, W), BF), gradient, gradi...]
where the time goes in v4:
time: 73.4 us; the launch traced here: 73.3 us
  Pallas kernels  72.6 us (99%)
    pallas_call x1, Pallas kernels, body(): pl.pallas_call(kernel, out_shape=(shape((E, BLK, W), BF), gradient, gradi...  69.2 us
    pallas_call x1, Pallas kernels, body(): pl.pallas_call(deliver, out_shape=(shape((T, D), BF), shape((1, T), F32),...  3.38 us

profile of v4, /device:TPU:1, one launch (start us, length us, event | category | flops | bytes accessed | tf_op | source)
XLA Modules:
  0.0 73.3 jit_solution(5116999320532783830)
XLA Ops:
  0.6 69.2 %shard_map.111 = (bf16[64,16,256]{2,1,0:T(8,128)(2,1)}, bf16[1,768,768]{2,1,0:T(8,128)(2,1)}, bf16[1,768,768]{2,1,0:T(8,128)(2,1)}) custom-call(bf16[256,768]{1,0:T(8,128)(2,1)} %tok_hbm.1, bf16[256,768]{1,0:T(8,128)(2,1)} %up_hbm.1, f32[1,256]{1,0:T(1,128)} %bitcast.4, s32[1,256]{1,0:T(1,128)} %bitcast.6, s32[1,256]{1,0:T(1,128)} %bitcast.8, ...), custom_call_target="tpu_custom_call" | custom-call | tf_op jit(solution)/shard_map/pallas_call | solution.py:374
  69.9 3.4 %shard_map.112 = (bf16[256,768]{1,0:T(8,128)(2,1)}, f32[1,256]{1,0:T(1,128)}, bf16[1,768,768]{2,1,0:T(8,128)(2,1)}, bf16[1,768,768]{2,1,0:T(8,128)(2,1)}) custom-call(bf16[64,16,256]{2,1,0:T(8,128)(2,1)} %get-tuple-element.11.ret_hbm, bf16[1,768,768]{2,1,0:T(8,128)(2,1)} %get-tuple-element.12.gin_hbm, bf16[1,768,768]{2,1,0:T(8,128)(2,1)} %get-tuple-element.13.gout_hbm, ...), custom_call_target="tpu_custom_call" | custom-call | tf_op jit(solution)/shard_map/pallas_call | solution.py:417

commit v5 on v4

--- a/solution.py
+++ b/solution.py
@@ -75,6 +75,19 @@
     z = 4 * half + zl
 
     x, y = ex // 16, ex // 4 % 4
+    def signal(semaphore, group, expert):
+        pl.semaphore_signal(semaphore, inc=1, device_id={"dp": group, "expert": expert}, device_id_type=MESH)
+
+    def signal_ring(semaphore):
+        for hop in range(1, 8):
+            there = (z + hop) % 8
+            signal(semaphore, there // 4 * 2 + core, ex - zl + there % 4)
+
+    barrier = pltpu.get_barrier_semaphore()
+    signal(barrier, half * 2 + 1 - core, ex)
+    for hop in range(1, 16):
+        signal(barrier, dp, (x + hop // 4) % 4 * 16 + (y + hop % 4) % 4 * 4 + zl)
+    signal_ring(barrier)
     loads = [
         pltpu.make_async_copy(source, target, in_sem.at[index])
         for index, (source, target) in enumerate(
@@ -90,26 +103,10 @@
     ]
     for load in loads:
         load.start()
-
-    def signal(semaphore, group, expert):
-        pl.semaphore_signal(semaphore, inc=1, device_id={"dp": group, "expert": expert}, device_id_type=MESH)
-
-    def signal_ring(semaphore):
-        for hop in range(1, 8):
-            there = (z + hop) % 8
-            signal(semaphore, there // 4 * 2 + core, ex - zl + there % 4)
-
-    barrier = pltpu.get_barrier_semaphore()
-    signal(barrier, half * 2 + 1 - core, ex)
-    for hop in range(1, 16):
-        signal(barrier, dp, (x + hop // 4) % 4 * 16 + (y + hop % 4) % 4 * 4 + zl)
-    signal_ring(barrier)
     for load in loads:
         load.wait()
     win_copy = pltpu.make_async_copy(win_hbm.at[0], win, w_sem.at[0])
     wout_copy = pltpu.make_async_copy(wout_hbm.at[0], wout, w_sem.at[1])
-    win_copy.start()
-    wout_copy.start()
 
     seg = seg_ref[...]
     weight = jnp.zeros((1, T), F32)
@@ -164,6 +161,8 @@
             near[0] = packed[0]
             pl.semaphore_wait(ready, 7)
         lax.fori_loop(max(1, g * GRP), (g + 1) * GRP, send_near, 0)
+    win_copy.start()
+    wout_copy.start()
     lax.fori_loop(0, FIRST, send_far, 0)
 
     spot = iota((GR, GRP * BLK), 0)
@@ -344,7 +343,7 @@
     slot_column = column(slot.astype(F32)).astype(I32)
     place = iota((T, E * BLK), 1) - code
     hots = [ones_where(place == slot_column + CAP * k) for k in range(D // W)]
-    gate_hot = ones_where(place == BLK - 1)
+    gate_hot = ones_where(iota((T, E), 1) * BLK == code)
     for load, store in zip(loads[4:], stores[:2]):
         load.wait()
         store.start()
@@ -353,7 +352,7 @@
     for k in range(D // W):
         dtok[:, k * W : (k + 1) * W] = nn(hots[k], returned).astype(BF)
     stores[2].start()
-    picked = nn(gate_hot, returned)
+    picked = nn(gate_hot, ret[:, BLK - 1, :])
     lane = iota((T, W), 1)
     picked = jnp.where((lane == slot_column) | (lane == slot_column + 128), picked, 0.0)
     sums = jnp.sum(picked, axis=1, keepdims=True)

time: 73.4 us -> 73.3 us (level)
  no operation moved by 1% of the time
where the time goes in v5:
time: 73.3 us; the launch traced here: 73.2 us
  Pallas kernels  72.5 us (99%)
    pallas_call x1, Pallas kernels, body(): pl.pallas_call(kernel, out_shape=(shape((E, BLK, W), BF), gradient, gradi...  69.2 us
    pallas_call x1, Pallas kernels, body(): pl.pallas_call(deliver, out_shape=(shape((T, D), BF), shape((1, T), F32),...  3.3 us

profile of v5, /device:TPU:1, one launch (start us, length us, event | category | flops | bytes accessed | tf_op | source)
XLA Modules:
  0.0 73.2 jit_solution(5016803042257255057)
XLA Ops:
  0.6 69.2 %shard_map.111 = (bf16[64,16,256]{2,1,0:T(8,128)(2,1)}, bf16[1,768,768]{2,1,0:T(8,128)(2,1)}, bf16[1,768,768]{2,1,0:T(8,128)(2,1)}) custom-call(bf16[256,768]{1,0:T(8,128)(2,1)} %tok_hbm.1, bf16[256,768]{1,0:T(8,128)(2,1)} %up_hbm.1, f32[1,256]{1,0:T(1,128)} %bitcast.4, s32[1,256]{1,0:T(1,128)} %bitcast.6, s32[1,256]{1,0:T(1,128)} %bitcast.8, ...), custom_call_target="tpu_custom_call" | custom-call | tf_op jit(solution)/shard_map/pallas_call | solution.py:373
  69.9 3.3 %shard_map.112 = (bf16[256,768]{1,0:T(8,128)(2,1)}, f32[1,256]{1,0:T(1,128)}, bf16[1,768,768]{2,1,0:T(8,128)(2,1)}, bf16[1,768,768]{2,1,0:T(8,128)(2,1)}) custom-call(bf16[64,16,256]{2,1,0:T(8,128)(2,1)} %get-tuple-element.11.ret_hbm, bf16[1,768,768]{2,1,0:T(8,128)(2,1)} %get-tuple-element.12.gin_hbm, bf16[1,768,768]{2,1,0:T(8,128)(2,1)} %get-tuple-element.13.gout_hbm, ...), custom_call_target="tpu_custom_call" | custom-call | tf_op jit(solution)/shard_map/pallas_call | solution.py:416
